TPU v7x, 32 devices: a whole 2x2x4 slice. The times are simulated.
32 devices in a mesh: vocab: 16 (over z, y, x), batch: 2 (over core).
Axes of the slice: x: 2, y: 2, z: 4, core: 2. Of those that a mesh axis runs over, the one named last changes fastest.
Arguments:
- hidden: bfloat16 [256, 4096], P('batch', 'vocab'), may hold values from -6 to 6
- head_weight: bfloat16 [4096, 65536], P('batch', 'vocab'), may hold values from -0.09375 to 0.09375
- passages: bfloat16 [512, 65536], P('batch', 'vocab'), may hold values from -6 to 6
- pair_query: int32 [768], P('batch'), may hold values from 0 to 15
- pair_passage: int32 [768], P('batch'), may hold values from 0 to 255
- pair_count: int32 [2], P('batch'), may hold values from 128 to 384, as said below
- teacher: float32 [768], P('batch'), may hold values from -24 to 24
Outputs:
- pooled: bfloat16 [16, 65536], P('batch', 'vocab')
- grad_hidden: bfloat16 [256, 4096], P('batch', 'vocab')
- loss_value: float32 [], replicated
Inputs may be any that keep to these rules, and one draw needn't show every extreme that they name: `pair_count`: slots of a group at or past its count are padding; some group has all 384 slots live.
All inputs are finite; a program needn't handle non-finite values.
Results may differ from a plain program's by a relative error of at most 0.012.
Values may be sent and summed in bfloat16 or wider, within the bound.
A program may use at most 128 MiB of HBM per device.

v0:
```python
import math

import jax
import jax.numpy as jnp
from jax import lax
from jax.sharding import PartitionSpec as P

VOCAB = 65536
QLEN = 16


def local(hidden, head_weight, passages, pair_query, pair_passage, pair_count, teacher):
    features = lax.all_gather(hidden, "vocab", axis=1, tiled=True)
    full_head = lax.all_gather(head_weight, "batch", axis=0, tiled=True)
    logits = jnp.dot(features, full_head, preferred_element_type=jnp.float32)
    positive = jnp.maximum(logits, 0.0)
    saturated = jnp.log1p(positive)
    tok_count, col_count = logits.shape
    query_count = tok_count // QLEN
    pooled = saturated.reshape(query_count, QLEN, col_count).sum(1).astype(jnp.bfloat16)
    every_query = lax.all_gather(pooled, "batch", axis=0, tiled=True)
    score_table = jnp.dot(every_query, passages.T, preferred_element_type=jnp.float32)
    partial_value = score_table[pair_query, pair_passage]
    inv_root = 1.0 / math.sqrt(VOCAB)
    slot_count = pair_query.shape[0]
    is_live = jnp.arange(slot_count, dtype=jnp.int32) < pair_count[0]
    scores = lax.psum(partial_value, "vocab") * inv_root
    residual = jnp.where(is_live, scores - teacher, 0.0)
    error_total = lax.psum(jnp.sum(residual * residual), "batch")
    pair_grad = 2.0 * residual * inv_root
    loss_value = error_total / (slot_count * lax.axis_size("batch"))
    query_onehot = (
        pair_query[:, None] == jnp.arange(every_query.shape[0], dtype=jnp.int32)[None, :]
    ).astype(jnp.float32)
    passage_onehot = (
        pair_passage[:, None] == jnp.arange(passages.shape[0], dtype=jnp.int32)[None, :]
    ).astype(jnp.float32)
    pair_table = jnp.dot(
        query_onehot.T, passage_onehot * pair_grad[:, None], precision=lax.Precision.HIGHEST
    )
    table_high = pair_table.astype(jnp.bfloat16)
    table_low = (pair_table - table_high.astype(jnp.float32)).astype(jnp.bfloat16)
    query_terms = jnp.dot(table_high, passages, preferred_element_type=jnp.float32) + jnp.dot(
        table_low, passages, preferred_element_type=jnp.float32
    )
    query_grad = lax.psum_scatter(query_terms, "batch", scatter_dimension=0, tiled=True)
    slope_term = jnp.where(logits > 0, 1.0 / (1.0 + positive), 0.0)
    spread_grad = jnp.broadcast_to(query_grad[:, None, :], (query_count, QLEN, col_count)).reshape(
        tok_count, col_count
    )
    logit_grad = (spread_grad * slope_term).astype(jnp.bfloat16)
    hidden_terms = lax.dot_general(
        logit_grad, full_head, (((1,), (1,)), ((), ())), preferred_element_type=jnp.float32
    )
    grad_hidden = lax.psum_scatter(hidden_terms, "vocab", scatter_dimension=1, tiled=True).astype(
        jnp.bfloat16
    )
    return (pooled, grad_hidden, loss_value)


def solution(mesh):
    in_specs = (
        P("batch", "vocab"),
        P("batch", "vocab"),
        P("batch", "vocab"),
        P("batch"),
        P("batch"),
        P("batch"),
        P("batch"),
    )
    out_specs = (P("batch", "vocab"), P("batch", "vocab"), P())
    return jax.shard_map(local, mesh=mesh, in_specs=in_specs, out_specs=out_specs, check_vma=False)
```

profile of v0, /device:TPU:0, one launch (start us, length us, event | category | flops | bytes accessed | tf_op | source)
XLA Modules:
  0.0 302.4 jit_solution(15925347458949185622)
XLA Ops:
  7.2 0.0 copy-start
  7.2 0.0 all-gather.3.cloned.1.call-start
  7.2 0.7 all-gather.3.cloned.1.call-update
  7.9 0.0 copy-start.3
  7.9 0.0 copy-start.4
  7.9 0.0 all-gather.5.cloned.1.call-start
  8.0 0.7 all-gather.5.cloned.1.call-update
  8.7 0.0 reduce-scatter.3.cloned.1.call-start
  9.4 0.0 copy-done.3
  9.4 0.0 copy-done.4
  9.4 59.2 %all-gather.3.cloned.1.call-done = bf16[128,4096]{1,0:T(8,128)(2,1)} async-done(((bf16[128,256]{1,0:T(8,128)(2,1)}), bf16[128,4096]{1,0:T(8,128)(2,1)}) %all-gather.3.cloned.1.call-update) | async-done | bytes 1048592 | tf_op jit(solution)/shard_map/all_gather | solution.py:13
  68.6 51.7 %all-gather.5.cloned.1.call-done = bf16[4096,4096]{1,0:T(8,128)(2,1)} async-done(((bf16[2048,4096]{1,0:T(8,128)(2,1)}), bf16[4096,4096]{1,0:T(8,128)(2,1)}) %all-gather.5.cloned.1.call-update) | async-done | bytes 33554448 | tf_op jit(solution)/shard_map/all_gather | solution.py:14
  120.2 17.7 %bitcast_reduce_fusion = (bf16[8,4096]{1,0:T(8,128)(2,1)S(1)}, f32[128,4096]{1,0:T(8,128)}) fusion(bf16[128,4096]{1,0:T(8,128)(2,1)} %all-gather.3.cloned.1.call-done, bf16[4096,4096]{1,0:T(8,128)(2,1)} %all-gather.5.cloned.1.call-done), kind=kOutput, calls=%fused_computation.4 | convolution fusion | flops 4295983104 | bytes 36765696 | tf_op jit(solution)/shard_map/dot_general | solution.py:15
  137.9 0.0 copy-start.1
  137.9 1.9 all_gather.11
  139.8 0.0 copy-done
  139.8 0.0 copy-start.2
  139.8 0.6 fusion.16
  140.5 3.5 %gather_fusion = f32[384]{0:T(512)S(1)} fusion(f32[16,256]{1,0:T(8,128)S(1)} %fusion.16, s32[384]{0:T(512)S(1)} %fusion.12), kind=kCustom, calls=%fused_computation | custom fusion | bytes 6144 | tf_op jit(solution)/shard_map/gather | solution.py:23
  143.9 0.0 copy-done.1
  144.0 42.0 %psum.14 = f32[384]{0:T(512)S(1)} all-reduce(f32[384]{0:T(512)S(1)} %gather_fusion), channel_id=1, replica_groups=mesh['vocab'=16,'batch'=2] {'vocab'}, use_global_device_ids=true, to_apply=%region_1.0 | all-reduce | flops 384 | bytes 3072 | tf_op jit(solution)/shard_map/psum | solution.py:27
  185.9 0.0 copy-done.2
  185.9 0.6 multiply_reduce_fusion
  186.5 0.5 fusion.1
  187.0 0.4 fusion.8
  187.4 1.1 convolution_add_fusion
  188.5 0.0 reduce-scatter.3.cloned.1.call-update
  188.5 0.0 reduce-scatter.5.cloned.1.call-start
  188.6 3.6 %reduce-scatter.3.cloned.1.call-done = f32[8,4096]{1,0:T(8,128)} async-done(((f32[16,4096]{1,0:T(8,128)}), f32[8,4096]{1,0:T(8,128)}) %reduce-scatter.3.cloned.1.call-update) | async-done | bytes 131088 | tf_op jit(solution)/shard_map/reduce_scatter | solution.py:46
  192.2 2.0 fusion
  194.3 17.2 %fusion.17 = f32[128,4096]{1,0:T(8,128)} fusion(bf16[128,4096]{1,0:T(8,128)(2,1)S(1)} %fusion, bf16[4096,4096]{1,0:T(8,128)(2,1)} %all-gather.5.cloned.1.call-done), kind=kOutput, calls=%fused_computation.31 | convolution fusion | flops 4294967296 | bytes 36700160 | tf_op jit(solution)/shard_map/dot_general | solution.py:52
  211.4 0.0 reduce-scatter.5.cloned.1.call-update
  211.4 3.1 %psum.15 = f32[]{:T(128)} all-reduce(f32[]{:T(128)} %get-tuple-element.3), channel_id=1, replica_groups=mesh['vocab'=16,'batch'=2] {'batch'}, use_global_device_ids=true, to_apply=%region_5.6 | all-reduce | flops 1 | bytes 8 | tf_op jit(solution)/shard_map/psum | solution.py:29
  215.2 78.0 %reduce-scatter.5.cloned.1.call-done = f32[128,256]{1,0:T(8,128)} async-done(((f32[128,4096]{1,0:T(8,128)}), f32[128,256]{1,0:T(8,128)}) %reduce-scatter.5.cloned.1.call-update) | async-done | bytes 131088 | tf_op jit(solution)/shard_map/reduce_scatter | solution.py:55
  293.2 1.5 convert_element_type.25
  (1 shorter events, 0.0 us)
Async XLA Ops:
  7.2 132.7 %copy-start = (bf16[256,4096]{1,0:T(8,128)(2,1)S(1)}, bf16[256,4096]{1,0:T(8,128)(2,1)}, u32[]{:S(2)}) copy-start(bf16[256,4096]{1,0:T(8,128)(2,1)} %param.9) | copy-start | bytes 6291460
  7.2 61.4 %all-gather.3.cloned.1.call-start = ((), (), s32[]{:S(2)}) async-start(), calls=%async_computation.2 | async-start | bytes 1114112 | tf_op jit(solution)/shard_map/all_gather | solution.py:13
  7.9 1.5 copy-start.3
  7.9 1.5 copy-start.4
  7.9 112.3 %all-gather.5.cloned.1.call-start = ((), (), s32[]{:S(2)}) async-start(), calls=%async_computation.3 | async-start | bytes 50331648 | tf_op jit(solution)/shard_map/all_gather | solution.py:14
  8.7 183.5 %reduce-scatter.3.cloned.1.call-start = ((), (), s32[]{:S(2)}) async-start(), calls=%async_computation.4 | async-start | bytes 393216 | tf_op jit(solution)/shard_map/reduce_scatter | solution.py:46
  137.9 6.0 %copy-start.1 = (bf16[8,4096]{1,0:T(8,128)(2,1)}, bf16[8,4096]{1,0:T(8,128)(2,1)S(1)}, u32[]{:S(2)}) copy-start(bf16[8,4096]{1,0:T(8,128)(2,1)S(1)} %get-tuple-element.5) | copy-start | bytes 196612
  139.8 46.1 %copy-start.2 = (f32[384]{0:T(512)S(1)}, f32[384]{0:T(512)}, u32[]{:S(2)}) copy-start(f32[384]{0:T(512)} %param.13) | copy-start | bytes 4612
  188.5 104.6 %reduce-scatter.5.cloned.1.call-start = ((), (), s32[]{:S(2)}) async-start(), calls=%async_computation.5 | async-start | bytes 2228224 | tf_op jit(solution)/shard_map/reduce_scatter | solution.py:55
Sparse Core Ops, SparseCore 0:
  10.7 57.7 all-gather.2
  70.1 50.0 all-gather.4
  188.7 3.5 reduce-scatter.2
  211.6 81.5 reduce-scatter.4
where the time goes:
time: 303 us; the launch traced here: 302 us
  waiting for transfers between devices  194 us (64%)
  blocking collectives  47 us (16%)
  matrix products  37.5 us (12%)
  between operations  16.3 us (5%)
  other arithmetic  4.19 us (1%)
  local copies, waits for them, and re-layouts  3.49 us (1%)
    reduce_scatter x1, waiting for transfers between devices, local(): lax.psum_scatter(hidden_terms, 'vocab', scatter_dimension=1, tiled=True)  78 us
    all_gather x1, waiting for transfers between devices, local(): features = lax.all_gather(hidden, 'vocab', axis=1, tiled=True)  59.2 us
    all_gather x1, waiting for transfers between devices, local(): full_head = lax.all_gather(head_weight, 'batch', axis=0, tiled=True)  51.7 us
    psum x1, blocking collectives, local(): scores = lax.psum(partial_value, 'vocab') * inv_root  42 us
    dot_general x1, matrix products, local(): logits = jnp.dot(features, full_head, preferred_element_type=jnp.float32)  17.7 us
    dot_general x1, matrix products, local(): lax.dot_general(logit_grad, full_head, (((1,), (1,)), ((), ())), preferre...  17.2 us
  transfers between devices with their start and end apart: 4, of which 4 were waited for; matrix products, arithmetic and copies ran while one was open for 0% of the time, Pallas kernels for 0%

commit v1 on v0

--- a/solution.py
+++ b/solution.py
@@ -1,15 +1,18 @@
+import functools
 import math
 
 import jax
 import jax.numpy as jnp
 from jax import lax
+from jax.experimental import pallas as pl
+from jax.experimental.pallas import tpu as pltpu
 from jax.sharding import PartitionSpec as P
 
 VOCAB = 65536
 QLEN = 16
 
 
-def local(hidden, head_weight, passages, pair_query, pair_passage, pair_count, teacher):
+def plain(hidden, head_weight, passages, pair_query, pair_passage, pair_count, teacher):
     features = lax.all_gather(hidden, "vocab", axis=1, tiled=True)
     full_head = lax.all_gather(head_weight, "batch", axis=0, tiled=True)
     logits = jnp.dot(features, full_head, preferred_element_type=jnp.float32)
@@ -58,6 +61,425 @@
     return (pooled, grad_hidden, loss_value)
 
 
+MESH = pl.DeviceIdType.MESH
+HIGHEST = lax.Precision.HIGHEST
+NT_DIMS = (((1,), (1,)), ((), ()))
+
+
+def device(v, b):
+    return (v, b)
+
+
+def landed(ref, sem):
+    pltpu.make_async_copy(ref, ref, sem).wait()
+
+
+def remote(src, dst, send, recv, to):
+    return pltpu.make_async_remote_copy(
+        src_ref=src, dst_ref=dst, send_sem=send, recv_sem=recv, device_id=to, device_id_type=MESH
+    )
+
+
+def kernel(
+    n_vocab, n_planes, n_in, tiles,
+    hid, head, pas, pair_q, pair_p, count, teacher,
+    pooled_out, grad_out, loss_out,
+    head_v, pas_v, feat, part, part_in, every_q, terms, terms_in, lgrad,
+    hidden_out, from_plane, plane_sum, from_column, plane_scores, column_scores, errors,
+    head_s, pas_s, col_send, feat_recv, plane_send, part_send, part_recv, pool_send, pool_recv,
+    terms_send, terms_recv, lgrad_send, lgrad_recv, ps_send, ps_recv, cs_send, cs_recv,
+    err_send, err_recv, x_send, x_recv, y_send, y_recv,
+):
+    tok, width = hid.shape
+    slots = pair_q.shape[1]
+    pg = pas.shape[0]
+    rows, cols = head.shape
+    ct = cols // tiles
+    blocks = rows // width
+    zb = blocks // n_in
+    queries = tok // QLEN
+    v, b = lax.axis_index("vocab"), lax.axis_index("batch")
+    z, r = v // n_in, v % n_in
+    other = 1 - b
+    peer = (v, other)
+    inv_root = 1.0 / math.sqrt(cols * n_vocab)
+
+    def plane_peer(s):
+        return (z * n_in + (r + s) % n_in, b)
+
+    def column_index(dz):
+        return ((z + dz) % n_planes) * n_in + r
+
+    def head_copy(t):
+        return pltpu.make_async_copy(
+            head.at[:, pl.ds(pl.multiple_of(t * ct, ct), ct)], head_v.at[t], head_s.at[t]
+        )
+
+    def pas_copy(t):
+        return pltpu.make_async_copy(
+            pas.at[:, pl.ds(pl.multiple_of(t * ct, ct), ct)], pas_v.at[t], pas_s.at[t]
+        )
+
+    barrier = pltpu.get_barrier_semaphore()
+    for s in range(1, n_in):
+        pl.semaphore_signal(barrier, inc=1, device_id=plane_peer(s), device_id_type=MESH)
+    for dz in range(n_planes):
+        if dz:
+            pl.semaphore_signal(barrier, inc=1, device_id=(column_index(dz), b), device_id_type=MESH)
+        pl.semaphore_signal(barrier, inc=1, device_id=(column_index(dz), other), device_id_type=MESH)
+
+    @pl.loop(0, tiles)
+    def _(t):
+        head_copy(t).start()
+
+    @pl.loop(0, tiles)
+    def _(t):
+        pas_copy(t).start()
+
+    pl.semaphore_wait(barrier, n_in - 1 + 2 * n_planes - 1)
+
+    def feat_at(j, half):
+        return feat.at[
+            pl.ds(pl.multiple_of(half * tok, tok), tok), pl.ds(pl.multiple_of(j * width, width), width)
+        ]
+
+    goal = v // blocks
+    mine = v % blocks
+
+    def column_copy(dz):
+        return remote(
+            hid, feat_at(mine, b), col_send.at[dz], feat_recv.at[mine * 2 + b], (column_index(dz), goal)
+        )
+
+    def own_feat():
+        return pltpu.make_async_copy(hid, feat_at(mine, b), feat_recv.at[mine * 2 + b])
+
+    def own_to_peer():
+        return remote(hid, feat_at(mine, b), col_send.at[0], feat_recv.at[mine * 2 + b], peer)
+
+    for dz in [2, 1, 3] if n_planes == 4 else range(1, n_planes):
+        column_copy(dz).start()
+
+    @pl.when(goal == b)
+    def _():
+        own_feat().start()
+
+    @pl.when(goal != b)
+    def _():
+        own_to_peer().start()
+
+    def plane_copy(zz, half, s):
+        j = zz * n_in + r
+        return remote(
+            feat_at(j, half),
+            feat_at(j, half),
+            plane_send.at[(zz * 2 + half) * (n_in - 1) + s - 1],
+            feat_recv.at[j * 2 + half],
+            plane_peer(s),
+        )
+
+    for zz in range(zb):
+        for half in range(2):
+            j = zz * n_in + r
+            landed(feat_at(j, half), feat_recv.at[j * 2 + half])
+            for s in range(1, n_in):
+                plane_copy(zz, half, s).start()
+    for zz in range(zb):
+        for half in range(2):
+            for s in range(1, n_in):
+                j = zz * n_in + (r + s) % n_in
+                landed(feat_at(j, half), feat_recv.at[j * 2 + half])
+
+    own_rows = pl.ds(pl.multiple_of(b * tok, tok), tok)
+    peer_rows = pl.ds(pl.multiple_of(other * tok, tok), tok)
+
+    def part_copy(t):
+        return remote(part.at[t, peer_rows], part_in.at[t], part_send.at[t], part_recv.at[t], peer)
+
+    @pl.loop(0, tiles)
+    def _(t):
+        head_copy(t).wait()
+        part[t] = jnp.dot(feat[...], head_v[t], preferred_element_type=jnp.float32)
+        part_copy(t).start()
+
+    def pool_copy(t):
+        return remote(every_q.at[b, t], every_q.at[b, t], pool_send.at[t], pool_recv.at[t], peer)
+
+    @pl.loop(0, tiles)
+    def _(t):
+        landed(part_in.at[t], part_recv.at[t])
+        logits = part[t, own_rows, :] + part_in[t]
+        part[t, own_rows, :] = logits
+        saturated = jnp.log1p(jnp.maximum(logits, 0.0))
+        pooled = saturated.reshape(queries, QLEN, ct).sum(1).astype(jnp.bfloat16)
+        pooled_out[:, pl.ds(pl.multiple_of(t * ct, ct), ct)] = pooled
+        every_q[b, t] = pooled.astype(jnp.float32)
+        pool_copy(t).start()
+
+    def table_step(t, table):
+        pas_copy(t).wait()
+        landed(every_q.at[other, t], pool_recv.at[t])
+        both = jnp.concatenate([every_q[0, t], every_q[1, t]], axis=0).astype(jnp.bfloat16)
+        return table + lax.dot_general(both, pas_v[t], NT_DIMS, preferred_element_type=jnp.float32)
+
+    table = lax.fori_loop(0, tiles, table_step, jnp.zeros((2 * queries, pg), jnp.float32))
+    hot_p = (pair_p[...] == lax.broadcasted_iota(jnp.int32, (pg, slots), 0)).astype(jnp.float32)
+    hot_q = (pair_q[...] == lax.broadcasted_iota(jnp.int32, (2 * queries, slots), 0)).astype(
+        jnp.float32
+    )
+    picked = jnp.dot(table, hot_p, precision=HIGHEST, preferred_element_type=jnp.float32)
+    plane_scores[r] = jnp.sum(picked * hot_q, axis=0, keepdims=True)
+
+    def plane_score_copy(s):
+        return remote(
+            plane_scores.at[r], plane_scores.at[r], ps_send.at[s - 1], ps_recv.at[r], plane_peer(s)
+        )
+
+    def column_score_copy(dz):
+        return remote(
+            column_scores.at[z], column_scores.at[z], cs_send.at[dz - 1], cs_recv.at[z],
+            (column_index(dz), b),
+        )
+
+    for s in range(1, n_in):
+        plane_score_copy(s).start()
+    for s in range(1, n_in):
+        landed(plane_scores.at[(r + s) % n_in], ps_recv.at[(r + s) % n_in])
+    column_scores[z] = jnp.sum(plane_scores[...], axis=0)
+    for dz in range(1, n_planes):
+        column_score_copy(dz).start()
+    for dz in range(1, n_planes):
+        landed(column_scores.at[(z + dz) % n_planes], cs_recv.at[(z + dz) % n_planes])
+    scores = jnp.sum(column_scores[...], axis=0) * inv_root
+
+    is_live = lax.broadcasted_iota(jnp.int32, (1, slots), 1) < count[...]
+    residual = jnp.where(is_live, scores - teacher[...], 0.0)
+    error = jnp.sum(residual * residual, axis=1, keepdims=True)
+    errors[b] = jnp.broadcast_to(error, errors.shape[1:])
+    err_copy = remote(errors.at[b], errors.at[b], err_send.at[0], err_recv.at[0], peer)
+    err_copy.start()
+    pair_grad = 2.0 * residual * inv_root
+    pair_table = lax.dot_general(
+        hot_q * pair_grad, hot_p, NT_DIMS, precision=HIGHEST, preferred_element_type=jnp.float32
+    )
+    high = pair_table.astype(jnp.bfloat16)
+    low = (pair_table - high.astype(jnp.float32)).astype(jnp.bfloat16)
+    split = jnp.concatenate([high, low], axis=0)
+
+    def terms_copy(t):
+        return remote(terms.at[other, t], terms_in.at[t], terms_send.at[t], terms_recv.at[t], peer)
+
+    @pl.loop(0, tiles)
+    def _(t):
+        both = jnp.dot(split, pas_v[t], preferred_element_type=jnp.float32)
+        whole = both[: 2 * queries] + both[2 * queries :]
+        terms[0, t] = whole[:queries]
+        terms[1, t] = whole[queries:]
+        terms_copy(t).start()
+
+    def lgrad_copy(t):
+        return remote(
+            lgrad.at[t, own_rows], lgrad.at[t, own_rows], lgrad_send.at[t], lgrad_recv.at[t], peer
+        )
+
+    @pl.loop(0, tiles)
+    def _(t):
+        landed(terms_in.at[t], terms_recv.at[t])
+        query_grad = terms[b, t] + terms_in[t]
+        logits = part[t, own_rows, :]
+        slope = jnp.where(logits > 0, 1.0 / (1.0 + jnp.maximum(logits, 0.0)), 0.0)
+        spread = jnp.broadcast_to(query_grad[:, None, :], (queries, QLEN, ct)).reshape(tok, ct)
+        lgrad[t, own_rows, :] = (spread * slope).astype(jnp.bfloat16)
+        lgrad_copy(t).start()
+
+    @pl.loop(0, tiles)
+    def _(t):
+        landed(lgrad.at[t, peer_rows], lgrad_recv.at[t])
+
+    def hidden_block(j):
+        block = pl.ds(pl.multiple_of(j * width, width), width)
+        total = jnp.zeros((2 * tok, width), jnp.float32)
+        for t in range(tiles):
+            total += lax.dot_general(
+                lgrad[t], head_v[t, block, :], NT_DIMS, preferred_element_type=jnp.float32
+            )
+        return total.reshape(2, tok, width)
+
+    def x_copy(zz, s):
+        return remote(
+            hidden_out.at[zz, s - 1],
+            from_plane.at[zz, s - 1],
+            x_send.at[zz * (n_in - 1) + s - 1],
+            x_recv.at[zz * (n_in - 1) + s - 1],
+            plane_peer(s),
+        )
+
+    @pl.loop(0, zb * (n_in - 1))
+    def _(i):
+        s, zz = n_in - 1 - i // zb, i % zb
+        hidden_out[zz, s - 1] = hidden_block(zz * n_in + (r + s) % n_in).astype(jnp.bfloat16)
+        x_copy(zz, s).start()
+
+    def y_copy(zz, half):
+        return remote(
+            plane_sum.at[zz, half],
+            from_column.at[z],
+            y_send.at[zz * 2 + half],
+            y_recv.at[z],
+            ((b * zb + zz) * n_in + r, half),
+        )
+
+    def y_here(zz, half):
+        return pltpu.make_async_copy(plane_sum.at[zz, half], from_column.at[z], y_recv.at[z])
+
+    def y_is_here(zz, half):
+        return jnp.logical_and(b * zb + zz == z, b == half)
+
+    @pl.loop(0, zb)
+    def _(zz):
+        total = hidden_block(zz * n_in + r)
+        for s in range(n_in - 1, 0, -1):
+            landed(from_plane.at[zz, s - 1], x_recv.at[zz * (n_in - 1) + s - 1])
+            total += from_plane[zz, s - 1].astype(jnp.float32)
+        plane_sum[zz] = total.astype(jnp.bfloat16)
+        for half in range(2):
+
+            @pl.when(y_is_here(zz, half))
+            def _():
+                y_here(zz, half).start()
+
+            @pl.when(jnp.logical_not(y_is_here(zz, half)))
+            def _():
+                y_copy(zz, half).start()
+
+    total = jnp.zeros((tok, width), jnp.float32)
+    for k in range(n_planes):
+        landed(from_column.at[k], y_recv.at[k])
+        total += from_column[k].astype(jnp.float32)
+    grad_out[...] = total.astype(jnp.bfloat16)
+
+    landed(errors.at[other], err_recv.at[0])
+    loss_out[...] = (errors[0] + errors[1]) / (slots * 2)
+
+    for dz in range(1, n_planes):
+        column_copy(dz).wait_send()
+        column_score_copy(dz).wait_send()
+
+    @pl.when(goal != b)
+    def _():
+        own_to_peer().wait_send()
+
+    for s in range(1, n_in):
+        plane_score_copy(s).wait_send()
+        for zz in range(zb):
+            x_copy(zz, s).wait_send()
+            for half in range(2):
+                plane_copy(zz, half, s).wait_send()
+    err_copy.wait_send()
+    for zz in range(zb):
+        for half in range(2):
+
+            @pl.when(jnp.logical_not(y_is_here(zz, half)))
+            def _():
+                y_copy(zz, half).wait_send()
+
+    @pl.loop(0, tiles)
+    def _(t):
+        part_copy(t).wait_send()
+        pool_copy(t).wait_send()
+        terms_copy(t).wait_send()
+        lgrad_copy(t).wait_send()
+
+
+def inner_axis(n_vocab):
+    size = 1
+    while size * size < n_vocab:
+        size *= 2
+    return size
+
+
+def fused(n_vocab, hidden, head_weight, passages, pair_query, pair_passage, pair_count, teacher):
+    tok, width = hidden.shape
+    rows, cols = head_weight.shape
+    pg = passages.shape[0]
+    slots = pair_query.shape[0]
+    n_in = inner_axis(n_vocab)
+    n_planes = n_vocab // n_in
+    blocks = rows // width
+    zb = blocks // n_in
+    ct = math.gcd(cols, 512)
+    tiles = cols // ct
+    queries = tok // QLEN
+    vmem = pl.BlockSpec(memory_space=pltpu.VMEM)
+    hbm = pl.BlockSpec(memory_space=pl.ANY)
+    bf16, f32 = jnp.bfloat16, jnp.float32
+    dma = pltpu.SemaphoreType.DMA
+    pooled, grad, loss = pl.pallas_call(
+        functools.partial(kernel, n_vocab, n_planes, n_in, tiles),
+        out_shape=(
+            jax.ShapeDtypeStruct((queries, cols), bf16),
+            jax.ShapeDtypeStruct((tok, width), bf16),
+            jax.ShapeDtypeStruct((1, 128), f32),
+        ),
+        in_specs=[vmem, hbm, hbm, vmem, vmem, vmem, vmem],
+        out_specs=(vmem, vmem, vmem),
+        scratch_shapes=[
+            pltpu.VMEM((tiles, rows, ct), bf16),
+            pltpu.VMEM((tiles, pg, ct), bf16),
+            pltpu.VMEM((2 * tok, rows), bf16),
+            pltpu.VMEM((tiles, 2 * tok, ct), f32),
+            pltpu.VMEM((tiles, tok, ct), f32),
+            pltpu.VMEM((2, tiles, queries, ct), f32),
+            pltpu.VMEM((2, tiles, queries, ct), f32),
+            pltpu.VMEM((tiles, queries, ct), f32),
+            pltpu.VMEM((tiles, 2 * tok, ct), bf16),
+            pltpu.VMEM((zb, n_in - 1, 2, tok, width), bf16),
+            pltpu.VMEM((zb, n_in - 1, 2, tok, width), bf16),
+            pltpu.VMEM((zb, 2, tok, width), bf16),
+            pltpu.VMEM((n_planes, tok, width), bf16),
+            pltpu.VMEM((n_in, 1, slots), f32),
+            pltpu.VMEM((n_planes, 1, slots), f32),
+            pltpu.VMEM((2, 1, 128), f32),
+            dma((tiles,)), dma((tiles,)),
+            dma((n_planes,)), dma((2 * blocks,)), dma((2 * zb * (n_in - 1),)),
+            dma((tiles,)), dma((tiles,)), dma((tiles,)), dma((tiles,)),
+            dma((tiles,)), dma((tiles,)), dma((tiles,)), dma((tiles,)),
+            dma((n_in - 1,)), dma((n_in,)), dma((n_planes - 1,)), dma((n_planes,)),
+            dma((1,)), dma((1,)),
+            dma((zb * (n_in - 1),)), dma((zb * (n_in - 1),)),
+            dma((2 * zb,)), dma((n_planes,)),
+        ],
+        compiler_params=pltpu.CompilerParams(
+            collective_id=0, has_side_effects=True, vmem_limit_bytes=52 * 1024 * 1024
+        ),
+        cost_estimate=pl.CostEstimate(
+            flops=8 * tok * rows * cols,
+            bytes_accessed=2 * rows * cols + 2 * pg * cols,
+            transcendentals=tok * cols,
+        ),
+    )(
+        hidden, head_weight, passages,
+        pair_query.reshape(1, slots), pair_passage.reshape(1, slots),
+        pair_count.reshape(1, 1), teacher.reshape(1, slots),
+    )
+    return (pooled, grad, loss[0, 0])
+
+
+def local(n_vocab, n_batch, hidden, head_weight, *rest):
+    width, rows, cols = hidden.shape[1], head_weight.shape[0], head_weight.shape[1]
+    n_in = inner_axis(n_vocab)
+    if (
+        n_batch == 2
+        and n_vocab % n_in == 0
+        and (rows // width) % n_in == 0
+        and width % 128 == 0
+        and cols % 512 == 0
+        and rows * cols <= 2**23
+    ):
+        return fused(n_vocab, hidden, head_weight, *rest)
+    return plain(hidden, head_weight, *rest)
+
+
 def solution(mesh):
     in_specs = (
         P("batch", "vocab"),
@@ -69,4 +491,6 @@
         P("batch"),
     )
     out_specs = (P("batch", "vocab"), P("batch", "vocab"), P())
-    return jax.shard_map(local, mesh=mesh, in_specs=in_specs, out_specs=out_specs, check_vma=False)
+    body = functools.partial(local, mesh.shape["vocab"], mesh.shape["batch"])
+    return jax.shard_map(
+        body, mesh=mesh, in_specs=in_specs, out_specs=out_specs, check_vma=False)

time: 303 us -> 70.7 us (0.23)
  waiting for transfers between devices: 194 us -> 0 us
  Pallas kernels: 0 us -> 63.5 us
  blocking collectives: 47 us -> 0 us
  matrix products: 37.5 us -> 0 us
  between operations: 16.3 us -> 2.45 us
  other arithmetic: 4.19 us -> 0 us
    all_gather x2 -> x0, waiting for transfers between devices: 111 us -> none  [the longest x1 59.2 us: local(): features = lax.all_gather(hidden, 'vocab', axis=1, tiled=True)]
    reduce_scatter x2 -> x0, waiting for transfers between devices: 81.6 us -> none  [the longest x1 78 us: local(): lax.psum_scatter(hidden_terms, 'vocab', scatter_dimension=1, tiled=True)]
    pallas_call x0 -> x1, Pallas kernels: none -> 63.5 us  [fused(): pl.pallas_call(functools.partial(kernel, n_vocab, n_planes, n_in, tiles),...]
    psum x2 -> x0, blocking collectives: 45.1 us -> none  [the longest x1 42 us: local(): scores = lax.psum(partial_value, 'vocab') * inv_root]
    dot_general x6 -> x0, matrix products: 37.5 us -> none  [the longest x1 17.7 us: local(): logits = jnp.dot(features, full_head, preferred_element_type=jnp.float32)]
    convert_element_type x2 -> x0, other arithmetic: 3.58 us -> none  [the longest x1 2.03 us: local(): logit_grad = (spread_grad * slope_term).astype(jnp.bfloat16)]
    gather x1 -> x0, local copies, waits for them, and re-layouts: 3.46 us -> none  [local(): partial_value = score_table[pair_query, pair_passage]]
  transfers between devices with their start and end apart: 4 -> 0, of which waited for: 4 -> 0; matrix products, arithmetic and copies ran while one was open for 0% -> 0% of each run, Pallas kernels for 0% -> 0%
where the time goes in v1:
time: 70.7 us; the launch traced here: 70.1 us
  Pallas kernels  63.5 us (90%)
  local copies, waits for them, and re-layouts  4.15 us (6%)
  between operations  2.45 us (3%)
    pallas_call x1, Pallas kernels, fused(): pl.pallas_call(functools.partial(kernel, n_vocab, n_planes, n_in, tiles),...  63.5 us
    unnamed x4, local copies, waits for them, and re-layouts  2.1 us

profile of v1, /device:TPU:0, one launch (start us, length us, event | category | flops | bytes accessed | tf_op | source)
XLA Modules:
  0.0 70.1 jit_solution(1489258311838864915)
XLA Ops:
  1.3 0.7 reshape.18.pair_q
  2.0 0.7 reshape.19.pair_p
  2.6 0.7 reshape.21.teacher
  3.3 0.0 copy-start
  3.3 0.8 %copy-done = bf16[128,256]{1,0:T(8,128)(2,1)S(1)} copy-done((bf16[128,256]{1,0:T(8,128)(2,1)S(1)}, bf16[128,256]{1,0:T(8,128)(2,1)}, u32[]{:S(2)}) %copy-start) | copy-done | bytes 65560
  4.2 63.5 %shard_map.94 = (bf16[8,4096]{1,0:T(8,128)(2,1)S(1)}, bf16[128,256]{1,0:T(8,128)(2,1)S(1)}, f32[1,128]{1,0:T(1,128)S(1)}) custom-call(bf16[128,256]{1,0:T(8,128)(2,1)S(1)} %copy-done, bf16[2048,4096]{1,0:T(8,128)(2,1)} %head.1, bf16[256,4096]{1,0:T(8,128)(2,1)} %pas.1, s32[1,384]{1,0:T(1,128)S(1)} %reshape.18.pair_q, s32[1,384]{1,0:T(1,128)S(1)} %reshape.19.pair_p, ...), custom_call_target="tpu_custom_call" | custom-call | flops 8589934592 | bytes 18874368 | tf_op jit(solution)/shard_map/pallas_call | solution.py:417
  67.7 0.6 copy.14
  68.3 0.6 copy.15
Async XLA Ops:
  3.3 0.8 %copy-start = (bf16[128,256]{1,0:T(8,128)(2,1)S(1)}, bf16[128,256]{1,0:T(8,128)(2,1)}, u32[]{:S(2)}) copy-start(bf16[128,256]{1,0:T(8,128)(2,1)} %hid.1) | copy-start | bytes 196612

commit v2 on v1

--- a/solution.py
+++ b/solution.py
@@ -85,13 +85,13 @@
     hid, head, pas, pair_q, pair_p, count, teacher,
     pooled_out, grad_out, loss_out,
     head_v, pas_v, feat, part, part_in, every_q, terms, terms_in, lgrad,
-    hidden_out, from_plane, plane_sum, from_column, plane_scores, column_scores, errors,
+    hidden_out, from_plane, own_sum, plane_sum, from_column, plane_scores, column_scores, errors,
     head_s, pas_s, col_send, feat_recv, plane_send, part_send, part_recv, pool_send, pool_recv,
     terms_send, terms_recv, lgrad_send, lgrad_recv, ps_send, ps_recv, cs_send, cs_recv,
     err_send, err_recv, x_send, x_recv, y_send, y_recv,
 ):
     tok, width = hid.shape
-    slots = pair_q.shape[1]
+    slots = pair_q.shape[0]
     pg = pas.shape[0]
     rows, cols = head.shape
     ct = cols // tiles
@@ -140,7 +140,9 @@
 
     def feat_at(j, half):
         return feat.at[
-            pl.ds(pl.multiple_of(half * tok, tok), tok), pl.ds(pl.multiple_of(j * width, width), width)
+            j // n_in,
+            pl.ds(pl.multiple_of(half * tok, tok), tok),
+            pl.ds(pl.multiple_of(j % n_in * width, width), width),
         ]
 
     goal = v // blocks
@@ -178,40 +180,67 @@
             plane_peer(s),
         )
 
-    for zz in range(zb):
+    first = jnp.clip(z - zb * b, 0, zb - 1)
+    for k in range(zb):
         for half in range(2):
+            zz = (first + k) % zb
             j = zz * n_in + r
             landed(feat_at(j, half), feat_recv.at[j * 2 + half])
             for s in range(1, n_in):
                 plane_copy(zz, half, s).start()
-    for zz in range(zb):
+
+    def plane_landed(zz):
         for half in range(2):
             for s in range(1, n_in):
                 j = zz * n_in + (r + s) % n_in
                 landed(feat_at(j, half), feat_recv.at[j * 2 + half])
 
+    def rows_product(zz, t):
+        deep = rows // zb
+        return jnp.dot(
+            feat[zz],
+            head_v[t, pl.ds(pl.multiple_of(zz * deep, deep), deep), :],
+            preferred_element_type=jnp.float32,
+        )
+
     own_rows = pl.ds(pl.multiple_of(b * tok, tok), tok)
     peer_rows = pl.ds(pl.multiple_of(other * tok, tok), tok)
 
     def part_copy(t):
         return remote(part.at[t, peer_rows], part_in.at[t], part_send.at[t], part_recv.at[t], peer)
 
-    @pl.loop(0, tiles)
-    def _(t):
-        head_copy(t).wait()
-        part[t] = jnp.dot(feat[...], head_v[t], preferred_element_type=jnp.float32)
+    for k in range(zb - 1):
+        zz = (first + k) % zb
+        plane_landed(zz)
+
+        @pl.loop(0, tiles)
+        def _(t):
+            if k == 0:
+                head_copy(t).wait()
+                part[t] = rows_product(zz, t)
+            else:
+                part[t] += rows_product(zz, t)
+
+    last = (first + zb - 1) % zb
+    plane_landed(last)
+
+    def produce(t):
+        if zb == 1:
+            head_copy(t).wait()
+            part[t] = rows_product(last, t)
+        else:
+            part[t] += rows_product(last, t)
         part_copy(t).start()
 
     def pool_copy(t):
         return remote(every_q.at[b, t], every_q.at[b, t], pool_send.at[t], pool_recv.at[t], peer)
 
-    @pl.loop(0, tiles)
-    def _(t):
+    def consume(t):
         landed(part_in.at[t], part_recv.at[t])
         logits = part[t, own_rows, :] + part_in[t]
-        part[t, own_rows, :] = logits
-        saturated = jnp.log1p(jnp.maximum(logits, 0.0))
-        pooled = saturated.reshape(queries, QLEN, ct).sum(1).astype(jnp.bfloat16)
+        positive = jnp.maximum(logits, 0.0)
+        part[t, own_rows, :] = jnp.where(logits > 0, 1.0 / (1.0 + positive), 0.0)
+        pooled = jnp.log1p(positive).reshape(queries, QLEN, ct).sum(1).astype(jnp.bfloat16)
         pooled_out[:, pl.ds(pl.multiple_of(t * ct, ct), ct)] = pooled
         every_q[b, t] = pooled.astype(jnp.float32)
         pool_copy(t).start()
@@ -222,9 +251,28 @@
         both = jnp.concatenate([every_q[0, t], every_q[1, t]], axis=0).astype(jnp.bfloat16)
         return table + lax.dot_general(both, pas_v[t], NT_DIMS, preferred_element_type=jnp.float32)
 
-    table = lax.fori_loop(0, tiles, table_step, jnp.zeros((2 * queries, pg), jnp.float32))
-    hot_p = (pair_p[...] == lax.broadcasted_iota(jnp.int32, (pg, slots), 0)).astype(jnp.float32)
-    hot_q = (pair_q[...] == lax.broadcasted_iota(jnp.int32, (2 * queries, slots), 0)).astype(
+    @pl.loop(0, 2)
+    def _(t):
+        produce(t)
+
+    produce(2)
+    consume(0)
+
+    def forward_step(t, table):
+        produce(t)
+        consume(t - 2)
+        return table_step(t - 3, table)
+
+    def tail_step(t, table):
+        consume(t)
+        return table_step(t - 1, table)
+
+    table = jnp.zeros((2 * queries, pg), jnp.float32)
+    table = lax.fori_loop(3, tiles, forward_step, table)
+    table = lax.fori_loop(tiles - 2, tiles, tail_step, table)
+    table = table_step(tiles - 1, table)
+    hot_p = (pair_p[...].reshape(1, slots) == lax.broadcasted_iota(jnp.int32, (pg, slots), 0)).astype(jnp.float32)
+    hot_q = (pair_q[...].reshape(1, slots) == lax.broadcasted_iota(jnp.int32, (2 * queries, slots), 0)).astype(
         jnp.float32
     )
     picked = jnp.dot(table, hot_p, precision=HIGHEST, preferred_element_type=jnp.float32)
@@ -252,8 +300,8 @@
         landed(column_scores.at[(z + dz) % n_planes], cs_recv.at[(z + dz) % n_planes])
     scores = jnp.sum(column_scores[...], axis=0) * inv_root
 
-    is_live = lax.broadcasted_iota(jnp.int32, (1, slots), 1) < count[...]
-    residual = jnp.where(is_live, scores - teacher[...], 0.0)
+    is_live = lax.broadcasted_iota(jnp.int32, (1, slots), 1) < count[0]
+    residual = jnp.where(is_live, scores - teacher[...].reshape(1, slots), 0.0)
     error = jnp.sum(residual * residual, axis=1, keepdims=True)
     errors[b] = jnp.broadcast_to(error, errors.shape[1:])
     err_copy = remote(errors.at[b], errors.at[b], err_send.at[0], err_recv.at[0], peer)
@@ -269,8 +317,7 @@
     def terms_copy(t):
         return remote(terms.at[other, t], terms_in.at[t], terms_send.at[t], terms_recv.at[t], peer)
 
-    @pl.loop(0, tiles)
-    def _(t):
+    def terms_step(t):
         both = jnp.dot(split, pas_v[t], preferred_element_type=jnp.float32)
         whole = both[: 2 * queries] + both[2 * queries :]
         terms[0, t] = whole[:queries]
@@ -282,15 +329,25 @@
             lgrad.at[t, own_rows], lgrad.at[t, own_rows], lgrad_send.at[t], lgrad_recv.at[t], peer
         )
 
-    @pl.loop(0, tiles)
-    def _(t):
+    def lgrad_step(t):
         landed(terms_in.at[t], terms_recv.at[t])
         query_grad = terms[b, t] + terms_in[t]
-        logits = part[t, own_rows, :]
-        slope = jnp.where(logits > 0, 1.0 / (1.0 + jnp.maximum(logits, 0.0)), 0.0)
         spread = jnp.broadcast_to(query_grad[:, None, :], (queries, QLEN, ct)).reshape(tok, ct)
-        lgrad[t, own_rows, :] = (spread * slope).astype(jnp.bfloat16)
+        lgrad[t, own_rows, :] = (spread * part[t, own_rows, :]).astype(jnp.bfloat16)
         lgrad_copy(t).start()
+
+    @pl.loop(0, 3)
+    def _(t):
+        terms_step(t)
+
+    @pl.loop(3, tiles)
+    def _(t):
+        terms_step(t)
+        lgrad_step(t - 3)
+
+    @pl.loop(tiles - 3, tiles)
+    def _(t):
+        lgrad_step(t)
 
     @pl.loop(0, tiles)
     def _(t):
@@ -316,7 +373,7 @@
 
     @pl.loop(0, zb * (n_in - 1))
     def _(i):
-        s, zz = n_in - 1 - i // zb, i % zb
+        s, zz = n_in - 1 - i % (n_in - 1), i // (n_in - 1)
         hidden_out[zz, s - 1] = hidden_block(zz * n_in + (r + s) % n_in).astype(jnp.bfloat16)
         x_copy(zz, s).start()
 
@@ -337,7 +394,11 @@
 
     @pl.loop(0, zb)
     def _(zz):
-        total = hidden_block(zz * n_in + r)
+        own_sum[zz] = hidden_block(zz * n_in + r)
+
+    @pl.loop(0, zb)
+    def _(zz):
+        total = own_sum[zz]
         for s in range(n_in - 1, 0, -1):
             landed(from_plane.at[zz, s - 1], x_recv.at[zz * (n_in - 1) + s - 1])
             total += from_plane[zz, s - 1].astype(jnp.float32)
@@ -421,12 +482,12 @@
             jax.ShapeDtypeStruct((tok, width), bf16),
             jax.ShapeDtypeStruct((1, 128), f32),
         ),
-        in_specs=[vmem, hbm, hbm, vmem, vmem, vmem, vmem],
+        in_specs=[vmem, hbm, hbm, vmem, vmem, pl.BlockSpec(memory_space=pltpu.SMEM), vmem],
         out_specs=(vmem, vmem, vmem),
         scratch_shapes=[
             pltpu.VMEM((tiles, rows, ct), bf16),
             pltpu.VMEM((tiles, pg, ct), bf16),
-            pltpu.VMEM((2 * tok, rows), bf16),
+            pltpu.VMEM((zb, 2 * tok, rows // zb), bf16),
             pltpu.VMEM((tiles, 2 * tok, ct), f32),
             pltpu.VMEM((tiles, tok, ct), f32),
             pltpu.VMEM((2, tiles, queries, ct), f32),
@@ -435,6 +496,7 @@
             pltpu.VMEM((tiles, 2 * tok, ct), bf16),
             pltpu.VMEM((zb, n_in - 1, 2, tok, width), bf16),
             pltpu.VMEM((zb, n_in - 1, 2, tok, width), bf16),
+            pltpu.VMEM((zb, 2, tok, width), f32),
             pltpu.VMEM((zb, 2, tok, width), bf16),
             pltpu.VMEM((n_planes, tok, width), bf16),
             pltpu.VMEM((n_in, 1, slots), f32),
@@ -459,8 +521,7 @@
         ),
     )(
         hidden, head_weight, passages,
-        pair_query.reshape(1, slots), pair_passage.reshape(1, slots),
-        pair_count.reshape(1, 1), teacher.reshape(1, slots),
+        pair_query, pair_passage, pair_count, teacher,
     )
     return (pooled, grad, loss[0, 0])
 
@@ -474,6 +535,7 @@
         and (rows // width) % n_in == 0
         and width % 128 == 0
         and cols % 512 == 0
+        and cols >= 2048
         and rows * cols <= 2**23
     ):
         return fused(n_vocab, hidden, head_weight, *rest)

time: 70.7 us -> 68.7 us (0.972)
  Pallas kernels: 63.5 us -> 61.8 us
    reshape x3 -> x0, local copies, waits for them, and re-layouts: 2.05 us -> none  [the longest x1 0.68 us: fused(): pair_query.reshape(1, slots)]
    unnamed x4 -> x10, local copies, waits for them, and re-layouts: 2.1 us -> 4.14 us
    pallas_call x1, Pallas kernels: 63.5 us -> 61.8 us  [fused(): pl.pallas_call(functools.partial(kernel, n_vocab, n_planes, n_in, tiles),...]
where the time goes in v2:
time: 68.7 us; the launch traced here: 68.4 us
  Pallas kernels  61.8 us (90%)
  local copies, waits for them, and re-layouts  4.14 us (6%)
  between operations  2.46 us (4%)
    pallas_call x1, Pallas kernels, fused(): pl.pallas_call(functools.partial(kernel, n_vocab, n_planes, n_in, tiles),...  61.8 us
    unnamed x10, local copies, waits for them, and re-layouts  4.14 us

profile of v2, /device:TPU:0, one launch (start us, length us, event | category | flops | bytes accessed | tf_op | source)
XLA Modules:
  0.0 68.4 jit_solution(3543325901817536456)
XLA Ops:
  1.3 0.0 copy-start
  1.3 0.8 %copy-done = bf16[128,256]{1,0:T(8,128)(2,1)S(1)} copy-done((bf16[128,256]{1,0:T(8,128)(2,1)S(1)}, bf16[128,256]{1,0:T(8,128)(2,1)}, u32[]{:S(2)}) %copy-start) | copy-done | bytes 65560
  2.1 0.0 copy-start.1
  2.1 0.7 copy-done.1
  2.8 0.0 copy-start.2
  2.8 0.7 copy-done.2
  3.5 0.0 copy-start.3
  3.5 0.7 copy-done.3
  4.2 61.8 %shard_map.94 = (bf16[8,4096]{1,0:T(8,128)(2,1)S(1)}, bf16[128,256]{1,0:T(8,128)(2,1)S(1)}, f32[1,128]{1,0:T(1,128)S(1)}) custom-call(bf16[128,256]{1,0:T(8,128)(2,1)S(1)} %copy-done, bf16[2048,4096]{1,0:T(8,128)(2,1)} %head.1, bf16[256,4096]{1,0:T(8,128)(2,1)} %pas.1, s32[384]{0:T(512)S(1)} %copy-done.1, s32[384]{0:T(512)S(1)} %copy-done.2, ...), custom_call_target="tpu_custom_call" | custom-call | flops 8589934592 | bytes 18874368 | tf_op jit(solution)/shard_map/pallas_call | solution.py:478
  66.0 0.6 copy.14
  66.6 0.6 copy.15
Async XLA Ops:
  1.3 0.8 %copy-start = (bf16[128,256]{1,0:T(8,128)(2,1)S(1)}, bf16[128,256]{1,0:T(8,128)(2,1)}, u32[]{:S(2)}) copy-start(bf16[128,256]{1,0:T(8,128)(2,1)} %hid.1) | copy-start | bytes 196612
  2.1 0.7 copy-start.1
  2.8 0.7 copy-start.2
  3.5 0.7 copy-start.3
